TPU v7x, 32 devices: a whole 2x2x4 slice. The times are simulated.
32 devices in a mesh: dp: 4 (over x, core), space: 8 (over z, y).
Axes of the slice: x: 2, y: 2, z: 4, core: 2. Of those that a mesh axis runs over, the one named last changes fastest.
Arguments:
- features: bfloat16 [4, 32, 256, 512], P('dp', None, 'space'), may hold values from -6 to 6
- cotangent: bfloat16 [4, 32, 256, 512], P('dp', None, 'space'), may hold values from -6 to 6
- conv_kernel: float32 [7, 7, 512], replicated, may hold values from -0.875 to 0.875
- conv_bias: float32 [512], replicated, may hold values from -3 to 3
- norm_gain: float32 [512], replicated, may hold values from 0.5 to 1.5
- norm_bias: float32 [512], replicated, may hold values from -3 to 3
- weight_in: bfloat16 [512, 2048], P(('dp', 'space')), may hold values from -0.25 to 0.25
- bias_in: float32 [2048], replicated, may hold values from -3 to 3
- weight_out: bfloat16 [2048, 512], P(('dp', 'space')), may hold values from -0.125 to 0.125
- bias_out: float32 [512], replicated, may hold values from -3 to 3
- layer_scale: float32 [512], replicated, may hold values from 0.3 to 1.5
Outputs:
- block_out: bfloat16 [4, 32, 256, 512], P('dp', None, 'space')
- grad_features: bfloat16 [4, 32, 256, 512], P('dp', None, 'space')
- grad_kernel: float32 [7, 7, 512], replicated
- grad_convbias: float32 [512], replicated
- grad_gain: float32 [512], replicated
- grad_normbias: float32 [512], replicated
- grad_inproj: float32 [512, 2048], P(('dp', 'space'))
- grad_inbias: float32 [2048], replicated
- grad_outproj: float32 [2048, 512], P(('dp', 'space'))
- grad_outbias: float32 [512], replicated
- grad_scale: float32 [512], replicated
All inputs are finite; a program needn't handle non-finite values.
Results may differ from a plain program's by a relative error of at most 0.009.
Values may be sent and summed in bfloat16 or wider, within the bound.
A program may use at most 576 MiB of HBM per device.

v0:
```python
import jax
import jax.numpy as jnp
from jax import lax
from jax.sharding import PartitionSpec as P

KS = 7
NORM_EPS = 1e-06


def padded_2(x, sides, width):
    for axis, dim in sides:
        peers, length = (lax.axis_size(axis), x.shape[dim])
        up = [(i, (i + 1) % peers) for i in range(peers - 1)]
        down = [(j, i) for i, j in up]
        last = lax.slice_in_dim(x, length - width, length, axis=dim)
        initial = lax.slice_in_dim(x, 0, width, axis=dim)
        before = lax.ppermute(last, axis, up)
        after = lax.ppermute(initial, axis, down)
        x = jnp.concatenate([before, x, after], axis=dim)
    return x


def gelu_exact(inputs):
    return jax.nn.gelu(inputs, approximate=False)


def conv_forward(padded, kernel, offset, row_count, col_count):
    summed = jnp.zeros((row_count, col_count, padded.shape[2]), jnp.float32)
    for tap_row in range(KS):
        for tap_col in range(KS):
            window = padded[tap_row : tap_row + row_count, tap_col : tap_col + col_count].astype(
                jnp.float32
            )
            summed = summed + kernel[tap_row, tap_col] * window
    return (summed + offset).astype(jnp.bfloat16)


def conv_backward(grad_padded, kernel, row_count, col_count):
    summed = jnp.zeros((row_count, col_count, grad_padded.shape[2]), jnp.float32)
    for tap_row in range(KS):
        for tap_col in range(KS):
            row_start = KS - 1 - tap_row
            col_start = KS - 1 - tap_col
            window = grad_padded[
                row_start : row_start + row_count, col_start : col_start + col_count
            ].astype(jnp.float32)
            summed = summed + kernel[tap_row, tap_col] * window
    return summed


def kernel_gradient(grad_conv, padded, row_count, col_count):
    grad_wide = grad_conv.astype(jnp.float32)
    taps = []
    for tap_row in range(KS):
        tap_line = []
        for tap_col in range(KS):
            window = padded[tap_row : tap_row + row_count, tap_col : tap_col + col_count].astype(
                jnp.float32
            )
            tap_line.append(jnp.sum(grad_wide * window, axis=(0, 1)))
        taps.append(jnp.stack(tap_line))
    return jnp.stack(taps)


def norm_mlp(
    conv_out,
    source,
    upstream,
    norm_gain,
    norm_bias,
    weight_in,
    bias_in,
    weight_out,
    bias_out,
    layer_scale,
):
    widened = conv_out.astype(jnp.float32)
    center = jnp.mean(widened, axis=-1, keepdims=True)
    shifted = widened - center
    inv_std = lax.rsqrt(jnp.mean(shifted * shifted, axis=-1, keepdims=True) + NORM_EPS)
    normed = shifted * inv_std
    activated = (normed * norm_gain + norm_bias).astype(jnp.bfloat16)
    pre_act = jnp.dot(activated, weight_in, preferred_element_type=jnp.float32) + bias_in
    hidden_wide, gelu_back = jax.vjp(gelu_exact, pre_act)
    hidden = hidden_wide.astype(jnp.bfloat16)
    branch = jnp.dot(hidden, weight_out, preferred_element_type=jnp.float32) + bias_out
    block_out = (source.astype(jnp.float32) + layer_scale * branch).astype(jnp.bfloat16)
    upstream_wide = upstream.astype(jnp.float32)
    d_branch = layer_scale * upstream_wide
    d_branch_b = d_branch.astype(jnp.bfloat16)
    grad_scale = jnp.sum(upstream_wide * branch, axis=0)
    grad_outbias = jnp.sum(d_branch, axis=0)
    grad_outproj = lax.dot_general(
        hidden, d_branch_b, (((0,), (0,)), ((), ())), preferred_element_type=jnp.float32
    )
    d_hidden = lax.dot_general(
        d_branch_b, weight_out, (((1,), (1,)), ((), ())), preferred_element_type=jnp.float32
    )
    d_pre = gelu_back(d_hidden)[0]
    d_pre_b = d_pre.astype(jnp.bfloat16)
    grad_inbias = jnp.sum(d_pre, axis=0)
    grad_inproj = lax.dot_general(
        activated, d_pre_b, (((0,), (0,)), ((), ())), preferred_element_type=jnp.float32
    )
    d_act = lax.dot_general(
        d_pre_b, weight_in, (((1,), (1,)), ((), ())), preferred_element_type=jnp.float32
    )
    grad_gain = jnp.sum(d_act * normed, axis=0)
    grad_normbias = jnp.sum(d_act, axis=0)
    scaled = d_act * norm_gain
    grad_conv = inv_std * (
        scaled
        - jnp.mean(scaled, axis=-1, keepdims=True)
        - normed * jnp.mean(scaled * normed, axis=-1, keepdims=True)
    )
    return (
        block_out,
        grad_conv.astype(jnp.bfloat16),
        (
            grad_gain,
            grad_normbias,
            grad_inproj,
            grad_inbias,
            grad_outproj,
            grad_outbias,
            grad_scale,
        ),
    )


def local(
    features,
    cotangent,
    conv_kernel,
    conv_bias,
    norm_gain,
    norm_bias,
    weight_in,
    bias_in,
    weight_out,
    bias_out,
    layer_scale,
):
    reach = KS // 2
    source = features[0]
    upstream = cotangent[0]
    row_count, col_count, channels = source.shape
    full_in, full_out = (
        lax.all_gather(weight_in, ("dp", "space"), axis=0, tiled=True),
        lax.all_gather(weight_out, ("dp", "space"), axis=0, tiled=True),
    )
    rimmed = padded_2(source, (("space", 1),), reach)
    padded = jnp.pad(rimmed, ((reach, reach), (0, 0), (0, 0)))
    conv_out = conv_forward(padded, conv_kernel, conv_bias, row_count, col_count)
    block_out, grad_conv, partials = norm_mlp(
        conv_out.reshape(-1, channels),
        source.reshape(-1, channels),
        upstream.reshape(-1, channels),
        norm_gain,
        norm_bias,
        full_in,
        bias_in,
        full_out,
        bias_out,
        layer_scale,
    )
    grad_conv = grad_conv.reshape(row_count, col_count, channels)
    grad_rimmed = padded_2(grad_conv, (("space", 1),), reach)
    grad_padded = jnp.pad(grad_rimmed, ((reach, reach), (0, 0), (0, 0)))
    conv_back = conv_backward(grad_padded, conv_kernel, row_count, col_count)
    grad_kern = kernel_gradient(grad_conv, padded, row_count, col_count)
    grad_cbias = jnp.sum(grad_conv.astype(jnp.float32), axis=(0, 1))
    grad_feat = (upstream.astype(jnp.float32) + conv_back).astype(jnp.bfloat16)
    grad_gain, grad_normbias, grad_inproj, grad_inbias, grad_outproj, grad_outbias, grad_scale = (
        partials
    )
    reduced = lax.psum(
        (grad_kern, grad_cbias, grad_gain, grad_normbias, grad_inbias, grad_outbias, grad_scale),
        ("dp", "space"),
    )
    owned_in, owned_out = (
        lax.psum_scatter(grad_inproj, ("dp", "space"), scatter_dimension=0, tiled=True),
        lax.psum_scatter(grad_outproj, ("dp", "space"), scatter_dimension=0, tiled=True),
    )
    return (
        block_out.reshape(1, row_count, col_count, channels),
        grad_feat[None],
        reduced[0],
        reduced[1],
        reduced[2],
        reduced[3],
        owned_in,
        reduced[4],
        owned_out,
        reduced[5],
        reduced[6],
    )


def solution(mesh):
    return jax.shard_map(
        local,
        mesh=mesh,
        in_specs=(
            P("dp", None, "space", None),
            P("dp", None, "space", None),
            P(),
            P(),
            P(),
            P(),
            P(("dp", "space"), None),
            P(),
            P(("dp", "space"), None),
            P(),
            P(),
        ),
        out_specs=(
            P("dp", None, "space", None),
            P("dp", None, "space", None),
            P(),
            P(),
            P(),
            P(),
            P(("dp", "space"), None),
            P(),
            P(("dp", "space"), None),
            P(),
            P(),
        ),
        check_vma=False,
    )
```

profile of v0, /device:TPU:0, one launch (start us, length us, event | category | flops | bytes accessed | tf_op | source)
XLA Modules:
  0.0 583.8 jit_solution(10404483312146317047)
XLA Ops:
  7.2 0.0 copy-start
  7.2 0.0 copy-start.8
  7.2 0.0 all-gather.3.cloned.1.call-start
  7.2 0.7 all-gather.3.cloned.1.call-update
  7.9 0.0 all-gather.5.cloned.1.call-start
  8.0 1.1 fusion.152
  9.1 4.9 collective-permute-start
  14.0 1.3 collective-permute-start.1
  15.3 0.0 all-gather.5.cloned.1.call-update
  15.3 0.0 all-reduce.5.cloned.1.call-start
  15.4 1.2 fusion.153
  16.5 1.1 fusion.154
  17.6 1.0 fusion.155
  18.6 0.0 collective-permute-done
  18.6 2.3 collective-permute-done.1
  20.9 2.0 select_maximum_fusion.2
  22.9 0.0 copy-done
  22.9 0.0 copy-done.8
  22.9 0.0 copy-start.7
  22.9 0.0 copy-start.10
  22.9 16.5 %convert_reduce_fusion.1 = (f32[32,32]{1,0:T(8,128)S(1)}, bf16[32,32,512]{2,1,0:T(8,128)(2,1)}) fusion(f32[512]{0:T(512)S(1)} %copy-done.8, bf16[38,38,512]{2,1,0:T(8,128)(2,1)S(1)} %select_maximum_fusion.2, f32[512]{0:T(512)S(1)} %bitcast.310, f32[512]{0:T(512)S(1)} %bitcast.312, f32[512]{0:T(512)S(1)} %bitcast.218, f32[512]{0:T(512)S(1)} %bitcast.220, ...), kind=kLoop, calls=%fused_computation.278 | loop fusion | flops 88079360 | bytes 46440448 | tf_op jit(solution)/shard_map/reduce_sum | solution.py:78
  39.4 0.1 div.15
  39.5 1.7 multiply_reduce_fusion.2
  41.2 0.1 rsqrt.12
  41.3 0.0 copy-done.7
  41.3 0.0 copy-done.10
  41.3 2.7 add_convert_fusion
  44.1 26.3 %all-gather.3.cloned.1.call-done = bf16[512,2048]{1,0:T(8,128)(2,1)} async-done(((bf16[16,2048]{1,0:T(8,128)(2,1)}), bf16[512,2048]{1,0:T(8,128)(2,1)}) %all-gather.3.cloned.1.call-update) | async-done | bytes 2097168 | tf_op jit(solution)/shard_map/all_gather | solution.py:149
  70.3 0.0 copy-done.13
  70.3 23.4 %multiply_convert_fusion = (bf16[1024,2048]{1,0:T(8,128)(2,1)}, f32[1024,2048]{1,0:T(8,128)}, f32[1024,2048]{1,0:T(8,128)}) fusion(f32[2048]{0:T(1024)S(1)} %copy-done.13, bf16[1024,512]{1,0:T(8,128)(2,1)} %add_convert_fusion, bf16[512,2048]{1,0:T(8,128)(2,1)} %all-gather.3.cloned.1.call-done), kind=kOutput, calls=%fused_computation.52 | convolution fusion | flops 2285895680 | bytes 24125440 | tf_op jit(solution)/shard_map/dot_general | solution.py:83
  93.7 35.0 %all-gather.5.cloned.1.call-done = bf16[2048,512]{1,0:T(8,128)(2,1)} async-done(((bf16[64,512]{1,0:T(8,128)(2,1)}), bf16[2048,512]{1,0:T(8,128)(2,1)}) %all-gather.5.cloned.1.call-update) | async-done | bytes 2097168 | tf_op jit(solution)/shard_map/all_gather | solution.py:150
  128.7 0.0 copy-done.9
  128.7 6.9 %fusion.134 = (f32[512]{0:T(512)S(1)}, bf16[1024,512]{1,0:T(8,128)(2,1)}, bf16[1024,512]{1,0:T(8,128)(2,1)S(1)}) fusion(bf16[1,32,32,512]{3,2,1,0:T(8,128)(2,1)} %param.12, f32[512]{0:T(512)S(1)} %copy-done.14, f32[512]{0:T(512)S(1)} %copy-done.9, bf16[1,32,32,512]{3,2,1,0:T(8,128)(2,1)S(1)} %copy-done, bf16[1024,2048]{1,0:T(8,128)(2,1)} %get-tuple-element.81, ...), kind=kOutput, calls=%fused_computation.251 | convolution fusion | flops 2152726016 | bytes 10491904 | tf_op jit(solution)/shard_map/dot_general | solution.py:86
  135.6 0.0 copy-start.2
  135.6 8.0 %fusion.156 = (f32[2048]{0:T(1024)S(1)}, bf16[1024,2048]{1,0:T(8,128)(2,1)S(1)}) fusion(f32[1024,2048]{1,0:T(8,128)S(1)} %copy-done.16, bf16[1024,512]{1,0:T(8,128)(2,1)S(1)} %get-tuple-element.87, bf16[2048,512]{1,0:T(8,128)(2,1)S(1)} %copy-done.12, f32[1024,2048]{1,0:T(8,128)} %get-tuple-element.141, f32[2048]{0:T(1024)S(1)} %copy-done.13), kind=kOutput, calls=%fused_computation.316 | convolution fusion | flops 2181036032 | bytes 24133632 | tf_op jit(solution)/shard_map/dot_general | solution.py:96
  143.7 2.9 multiply_reduce_fusion
  146.5 0.0 copy-start.1
  146.6 6.6 %fusion.129 = (f32[512]{0:T(512)S(1)}, f32[512]{0:T(512)S(1)}, f32[512]{0:T(512)S(1)}, f32[512]{0:T(512)S(1)}, f32[512]{0:T(512)S(1)}, /*index=5*/f32[512]{0:T(5...) fusion(bf16[38,38,512]{2,1,0:T(8,128)(2,1)S(1)} %select_maximum, ...), kind=kLoop, calls=%fused_computation.242 | loop fusion | flops 33545216 | bytes 23123968 | tf_op jit(solution)/shard_map/reduce_sum | solution.py:60
  153.1 0.5 convert_reduce_fusion
  153.6 5.2 fusion.111
  158.8 4.2 fusion.108
  163.4 0.0 copy-start.6
  163.4 0.6 copy-done.6
  164.0 0.0 all-reduce.5.cloned.1.call-update
  164.0 0.3 reduce-scatter.5.cloned.1.call-start
  164.3 6.8 %fusion.157 = f32[2048,512]{1,0:T(8,128)} fusion(bf16[1024,2048]{1,0:T(8,128)(2,1)} %get-tuple-element.81, bf16[1024,512]{1,0:T(8,128)(2,1)} %copy-done.15), kind=kOutput, calls=%fused_computation.317 | convolution fusion | flops 2147483648 | bytes 9437184 | tf_op jit(solution)/shard_map/dot_general | solution.py:93
  171.1 0.0 reduce-scatter.5.cloned.1.call-update
  171.2 0.0 reduce-scatter.3.cloned.1.call-start
  171.2 1.2 copy-done.4
  172.4 6.6 %fusion.136 = f32[512,2048]{1,0:T(8,128)} fusion(bf16[1024,512]{1,0:T(8,128)(2,1)S(1)} %copy-done.4, bf16[1024,2048]{1,0:T(8,128)(2,1)} %copy-done.3), kind=kOutput, calls=%fused_computation.257 | convolution fusion | flops 2147483648 | bytes 9437184 | tf_op jit(solution)/shard_map/dot_general | solution.py:102
  178.9 0.0 reduce-scatter.3.cloned.1.call-update
  179.0 0.1 fusion.151
  179.1 3.5 collective-permute-start.2
  182.6 1.3 collective-permute-start.3
  183.9 0.3 fusion.132
  184.2 41.0 %all-reduce.2 = (f32[512]{0:T(512)}, f32[512]{0:T(512)}, f32[512]{0:T(512)}, f32[2048]{0:T(1024)}, f32[512]{0:T(512)}, /*index=5*/f32[512]{0:T(512)}) all-reduce(f32[512]{0:T(512)S(1)} %get-tuple-element.66, f32[512]{0:T(512)S(1)} %get-tuple-element.11, ...), channel_id=1, replica_groups=mesh['dp'=4,'space'=8] {'dp','space'}, use_global_device_ids=true, to_apply=%region_55.56 | all-reduce | flops 4608 | bytes 36864 | tf_op jit(solution)/shard_map/psum | solution.py:177
  225.2 0.0 collective-permute-done.2
  225.2 0.0 collective-permute-done.3
  225.2 0.8 select_maximum_fusion
  226.0 16.7 %fusion.149 = bf16[1,32,32,512]{3,2,1,0:T(8,128)(2,1)} fusion(bf16[38,38,512]{2,1,0:T(8,128)(2,1)S(1)} %select_maximum_fusion, f32[512]{0:T(512)S(1)} %bitcast.311, f32[512]{0:T(512)S(1)} %bitcast.313, f32[512]{0:T(512)S(1)} %bitcast.219, f32[512]{0:T(512)S(1)} %bitcast.221, f32[512]{0:T(512)S(1)} %bitcast.223, f32[512]{0:T(512)S(1)} %bitcast.225, ...), kind=kLoop, calls=%fused_computation.299 | loop fusion | flops 87556096 | bytes 47482880 | tf_op jit(solution)/shard_map/broadcast_in_dim | solution.py:187
  242.7 41.1 %all-reduce.5.cloned.1.call-done = f32[7,7,512]{2,1,0:T(8,128)} async-done(((f32[7,7,512]{2,1,0:T(8,128)}), f32[7,7,512]{2,1,0:T(8,128)}) %all-reduce.5.cloned.1.call-update) | async-done | bytes 100368 | tf_op jit(solution)/shard_map/psum | solution.py:177
  283.8 147.9 %reduce-scatter.5.cloned.1.call-done = f32[64,512]{1,0:T(8,128)} async-done(((f32[2048,512]{1,0:T(8,128)}), f32[64,512]{1,0:T(8,128)}) %reduce-scatter.5.cloned.1.call-update) | async-done | bytes 131088 | tf_op jit(solution)/shard_map/reduce_scatter | solution.py:183
  431.7 144.1 %reduce-scatter.3.cloned.1.call-done = f32[16,2048]{1,0:T(8,128)} async-done(((f32[512,2048]{1,0:T(8,128)}), f32[16,2048]{1,0:T(8,128)}) %reduce-scatter.3.cloned.1.call-update) | async-done | bytes 131088 | tf_op jit(solution)/shard_map/reduce_scatter | solution.py:182
  575.8 1.6 copy.29
  (36 shorter events, 0.3 us)
Async XLA Ops:
  7.2 15.7 %copy-start = (bf16[1,32,32,512]{3,2,1,0:T(8,128)(2,1)S(1)}, bf16[1,32,32,512]{3,2,1,0:T(8,128)(2,1)}, u32[]{:S(2)}) copy-start(bf16[1,32,32,512]{3,2,1,0:T(8,128)(2,1)} %param.11) | copy-start | bytes 3145732
  7.2 15.7 %copy-start.8 = (f32[512]{0:T(512)S(1)}, f32[512]{0:T(512)}, u32[]{:S(2)}) copy-start(f32[512]{0:T(512)} %param.14) | copy-start | bytes 6148
  7.2 63.1 %all-gather.3.cloned.1.call-start = ((), (), s32[]{:S(2)}) async-start(), calls=%async_computation.2 | async-start | bytes 2162688 | tf_op jit(solution)/shard_map/all_gather | solution.py:149
  7.9 120.8 %all-gather.5.cloned.1.call-start = ((), (), s32[]{:S(2)}) async-start(), calls=%async_computation.3 | async-start | bytes 2162688 | tf_op jit(solution)/shard_map/all_gather | solution.py:150
  9.1 9.5 %collective-permute-start = (bf16[32,3,512]{2,1,0:T(4,128)(2,1)S(1)}, bf16[32,3,512]{2,1,0:T(4,128)(2,1)S(1)}, u32[]{:S(2)}, u32[]{:S(2)}) collective-permute-start(bf16[32,3,512]{2,1,0:T(4,128)(2,1)S(1)} %get-tuple-element.90), channel_id=1, source_target_pairs={{0,1},{1,2},{2,3},{3,4},{4,5},{5,6},{6,7},{8,9},{9,10},{10,11},{11... | collective-permute-start | bytes 294920 | tf_op jit(solution)/shard_map/ppermute | solution.py:17
  14.0 6.9 %collective-permute-start.1 = (bf16[32,3,512]{2,1,0:T(4,128)(2,1)S(1)}, bf16[32,3,512]{2,1,0:T(4,128)(2,1)S(1)}, u32[]{:S(2)}, u32[]{:S(2)}) collective-permute-start(bf16[32,3,512]{2,1,0:T(4,128)(2,1)S(1)} %get-tuple-element.91), channel_id=1, source_target_pairs={{1,0},{2,1},{3,2},{4,3},{5,4},{6,5},{7,6},{9,8},{10,9},{11,10},{12... | collective-permute-start | bytes 294920 | tf_op jit(solution)/shard_map/ppermute | solution.py:18
  15.3 268.5 %all-reduce.5.cloned.1.call-start = ((), (), s32[]{:S(2)}) async-start(), calls=%async_computation.4 | async-start | bytes 229376 | tf_op jit(solution)/shard_map/psum | solution.py:177
  22.9 18.4 %copy-start.7 = (f32[512]{0:T(512)S(1)}, f32[512]{0:T(512)}, u32[]{:S(2)}) copy-start(f32[512]{0:T(512)} %param.15) | copy-start | bytes 6148
  22.9 18.4 %copy-start.10 = (f32[512]{0:T(512)S(1)}, f32[512]{0:T(512)}, u32[]{:S(2)}) copy-start(f32[512]{0:T(512)} %param.16) | copy-start | bytes 6148
  39.4 30.9 %copy-start.13 = (f32[2048]{0:T(1024)S(1)}, f32[2048]{0:T(1024)}, u32[]{:S(2)}) copy-start(f32[2048]{0:T(1024)} %param.18) | copy-start | bytes 24580
  44.1 84.7 %copy-start.9 = (f32[512]{0:T(512)S(1)}, f32[512]{0:T(512)}, u32[]{:S(2)}) copy-start(f32[512]{0:T(512)} %param.21) | copy-start | bytes 6148
  44.1 84.7 %copy-start.14 = (f32[512]{0:T(512)S(1)}, f32[512]{0:T(512)}, u32[]{:S(2)}) copy-start(f32[512]{0:T(512)} %param.20) | copy-start | bytes 6148
  128.7 6.9 %copy-start.12 = (bf16[2048,512]{1,0:T(8,128)(2,1)S(1)}, bf16[2048,512]{1,0:T(8,128)(2,1)}, u32[]{:S(2)}) copy-start(bf16[2048,512]{1,0:T(8,128)(2,1)} %all-gather.5.cloned.1.call-done) | copy-start | bytes 6291460
  128.7 6.9 %copy-start.16 = (f32[1024,2048]{1,0:T(8,128)S(1)}, f32[1024,2048]{1,0:T(8,128)}, u32[]{:S(2)}) copy-start(f32[1024,2048]{1,0:T(8,128)} %get-tuple-element.82) | copy-start | bytes 25165828
  135.6 8.0 %copy-start.15 = (bf16[1024,512]{1,0:T(8,128)(2,1)}, bf16[1024,512]{1,0:T(8,128)(2,1)S(1)}, u32[]{:S(2)}) copy-start(bf16[1024,512]{1,0:T(8,128)(2,1)S(1)} %get-tuple-element.87) | copy-start | bytes 3145732
  135.6 8.0 %copy-start.2 = (bf16[32,32,512]{2,1,0:T(8,128)(2,1)S(1)}, bf16[32,32,512]{2,1,0:T(8,128)(2,1)}, u32[]{:S(2)}) copy-start(bf16[32,32,512]{2,1,0:T(8,128)(2,1)} %get-tuple-element.84) | copy-start | bytes 3145732
  135.6 8.0 %copy-start.11 = (bf16[512,2048]{1,0:T(8,128)(2,1)S(1)}, bf16[512,2048]{1,0:T(8,128)(2,1)}, u32[]{:S(2)}) copy-start(bf16[512,2048]{1,0:T(8,128)(2,1)} %all-gather.3.cloned.1.call-done) | copy-start | bytes 6291460
  143.6 2.9 copy-start.3
  146.5 6.6 %copy-start.1 = (bf16[1,32,32,512]{3,2,1,0:T(8,128)(2,1)S(1)}, bf16[1,32,32,512]{3,2,1,0:T(8,128)(2,1)}, u32[]{:S(2)}) copy-start(bf16[1,32,32,512]{3,2,1,0:T(8,128)(2,1)} %param.11) | copy-start | bytes 3145732
  163.4 0.6 copy-start.6
  164.0 267.6 %reduce-scatter.5.cloned.1.call-start = ((), (), s32[]{:S(2)}) async-start(), calls=%async_computation.6 | async-start | bytes 4325376 | tf_op jit(solution)/shard_map/reduce_scatter | solution.py:183
  171.1 1.2 copy-start.4
  171.2 404.6 %reduce-scatter.3.cloned.1.call-start = ((), (), s32[]{:S(2)}) async-start(), calls=%async_computation.5 | async-start | bytes 4325376 | tf_op jit(solution)/shard_map/reduce_scatter | solution.py:182
  178.9 4.9 copy-start.5
  179.1 46.1 %collective-permute-start.2 = (bf16[32,3,512]{2,1,0:T(4,128)(2,1)S(1)}, bf16[32,3,512]{2,1,0:T(4,128)(2,1)S(1)}, u32[]{:S(2)}, u32[]{:S(2)}) collective-permute-start(bf16[32,3,512]{2,1,0:T(4,128)(2,1)S(1)} %get-tuple-element.88), channel_id=1, source_target_pairs={{0,1},{1,2},{2,3},{3,4},{4,5},{5,6},{6,7},{8,9},{9,10},{10,11},{11... | collective-permute-start | bytes 294920 | tf_op jit(solution)/shard_map/ppermute | solution.py:17
  182.6 42.6 %collective-permute-start.3 = (bf16[32,3,512]{2,1,0:T(4,128)(2,1)S(1)}, bf16[32,3,512]{2,1,0:T(4,128)(2,1)S(1)}, u32[]{:S(2)}, u32[]{:S(2)}) collective-permute-start(bf16[32,3,512]{2,1,0:T(4,128)(2,1)S(1)} %get-tuple-element.89), channel_id=1, source_target_pairs={{1,0},{2,1},{3,2},{4,3},{5,4},{6,5},{7,6},{9,8},{10,9},{11,10},{12... | collective-permute-start | bytes 294920 | tf_op jit(solution)/shard_map/ppermute | solution.py:18
Sparse Core Ops, SparseCore 0:
  11.0 59.2 all-gather.2
  73.3 55.3 all-gather.4
  164.2 119.5 all-reduce.4
  286.5 145.1 reduce-scatter.4
  434.4 141.3 reduce-scatter.2
where the time goes:
time: 585 us; the launch traced here: 584 us
  waiting for transfers between devices  397 us (68%)
  other arithmetic  57.2 us (10%)
  matrix products  54.5 us (9%)
  blocking collectives  41 us (7%)
  between operations  14.1 us (2%)
  starting transfers between devices  11.4 us (2%)
  local copies, waits for them, and re-layouts  8.29 us (1%)
    reduce_scatter x1, waiting for transfers between devices, local(): lax.psum_scatter(grad_outproj, ('dp', 'space'), scatter_dimension=0, tile...  148 us
    reduce_scatter x1, waiting for transfers between devices, local(): lax.psum_scatter(grad_inproj, ('dp', 'space'), scatter_dimension=0, tiled...  144 us
    psum x1, waiting for transfers between devices, local(): lax.psum((grad_kern, grad_cbias, grad_gain, grad_normbias, grad_inbias, g...  41.1 us
    psum x1, blocking collectives, local(): lax.psum((grad_kern, grad_cbias, grad_gain, grad_normbias, grad_inbias, g...  41 us
    all_gather x1, waiting for transfers between devices, local(): lax.all_gather(weight_out, ('dp', 'space'), axis=0, tiled=True)  35 us
    all_gather x1, waiting for transfers between devices, local(): lax.all_gather(weight_in, ('dp', 'space'), axis=0, tiled=True)  26.3 us
    dot_general x1, matrix products, norm_mlp(): jnp.dot(activated, weight_in, preferred_element_type=jnp.float32) + bias_in  23.4 us
    broadcast_in_dim x1, other arithmetic, local(): grad_feat[None]  16.7 us
  transfers between devices with their start and end apart: 9, of which 6 were waited for; matrix products, arithmetic and copies ran while one was open for 14% of the time, Pallas kernels for 0%

commit v1 on v0

--- a/solution.py
+++ b/solution.py
@@ -175,8 +175,19 @@
         partials
     )
     reduced = lax.psum(
-        (grad_kern, grad_cbias, grad_gain, grad_normbias, grad_inbias, grad_outbias, grad_scale),
-        ("dp", "space"),
+        lax.psum(
+            (
+                grad_kern,
+                grad_cbias,
+                grad_gain,
+                grad_normbias,
+                grad_inbias,
+                grad_outbias,
+                grad_scale,
+            ),
+            "space",
+        ),
+        "dp",
     )
     owned_in, owned_out = (
         lax.psum_scatter(grad_inproj, ("dp", "space"), scatter_dimension=0, tiled=True),

time: 585 us -> 565 us (0.966)
  waiting for transfers between devices: 397 us -> 369 us
  blocking collectives: 41 us -> 48.8 us
    reduce_scatter x1, waiting for transfers between devices: 148 us -> 93.1 us  [local(): lax.psum_scatter(grad_outproj, ('dp', 'space'), scatter_dimension=0, tile...]
    psum x1, waiting for transfers between devices: 41.1 us -> 68 us  [local(): lax.psum((grad_kern, grad_cbias, grad_gain, grad_normbias, grad_inbias, g...]
    psum x0 -> x1, blocking collectives: none -> 11.2 us  [local(): lax.psum(lax.psum((grad_kern, grad_cbias, grad_gain, grad_normbias, grad_...]
  transfers between devices with their start and end apart: 9 -> 10, of which waited for: 6 -> 6; matrix products, arithmetic and copies ran while one was open for 14% -> 15% of each run, Pallas kernels for 0% -> 0%
where the time goes in v1:
time: 565 us
  waiting for transfers between devices  369 us (65%)
  other arithmetic  58.3 us (10%)
  matrix products  54.5 us (10%)
  blocking collectives  48.8 us (9%)
  between operations  14.5 us (3%)
  starting transfers between devices  11.3 us (2%)
  local copies, waits for them, and re-layouts  8.29 us (1%)
    reduce_scatter x1, waiting for transfers between devices, local(): lax.psum_scatter(grad_inproj, ('dp', 'space'), scatter_dimension=0, tiled...  144 us
    reduce_scatter x1, waiting for transfers between devices, local(): lax.psum_scatter(grad_outproj, ('dp', 'space'), scatter_dimension=0, tile...  93.1 us
    psum x1, waiting for transfers between devices, local(): lax.psum((grad_kern, grad_cbias, grad_gain, grad_normbias, grad_inbias, g...  68 us
    psum x1, blocking collectives, local(): lax.psum((grad_kern, grad_cbias, grad_gain, grad_normbias, grad_inbias, g...  37.6 us
    all_gather x1, waiting for transfers between devices, local(): lax.all_gather(weight_out, ('dp', 'space'), axis=0, tiled=True)  35 us
    all_gather x1, waiting for transfers between devices, local(): lax.all_gather(weight_in, ('dp', 'space'), axis=0, tiled=True)  26.3 us
    dot_general x1, matrix products, norm_mlp(): jnp.dot(activated, weight_in, preferred_element_type=jnp.float32) + bias_in  23.4 us
    broadcast_in_dim x1, other arithmetic, local(): grad_feat[None]  17.8 us
  transfers between devices with their start and end apart: 10, of which 6 were waited for; matrix products, arithmetic and copies ran while one was open for 15% of the time, Pallas kernels for 0%

profile of v1, /device:TPU:0, one launch (start us, length us, event | category | flops | bytes accessed | tf_op | source)
XLA Modules:
  0.0 564.7 jit_solution(11321310373579083791)
XLA Ops:
  7.2 0.0 copy-start
  7.2 0.0 copy-start.8
  7.2 0.0 all-gather.3.cloned.1.call-start
  7.2 0.7 all-gather.3.cloned.1.call-update
  7.9 0.0 all-gather.5.cloned.1.call-start
  8.0 1.1 fusion.152
  9.1 4.9 collective-permute-start
  14.0 1.3 collective-permute-start.1
  15.3 0.0 all-gather.5.cloned.1.call-update
  15.3 0.0 all-reduce.7.cloned.1.call-start
  15.4 1.2 fusion.153
  16.5 1.1 fusion.154
  17.6 1.0 fusion.155
  18.6 0.0 collective-permute-done
  18.6 2.3 collective-permute-done.1
  20.9 2.0 select_maximum_fusion.2
  22.9 0.0 copy-done
  22.9 0.0 copy-start.7
  22.9 0.0 copy-start.10
  22.9 16.5 %convert_reduce_fusion.1 = (f32[32,32]{1,0:T(8,128)S(1)}, bf16[32,32,512]{2,1,0:T(8,128)(2,1)}) fusion(f32[512]{0:T(512)S(1)} %copy-done.8, bf16[38,38,512]{2,1,0:T(8,128)(2,1)S(1)} %select_maximum_fusion.2, f32[512]{0:T(512)S(1)} %bitcast.310, f32[512]{0:T(512)S(1)} %bitcast.312, f32[512]{0:T(512)S(1)} %bitcast.218, f32[512]{0:T(512)S(1)} %bitcast.220, ...), kind=kLoop, calls=%fused_computation.278 | loop fusion | flops 88079360 | bytes 46440448 | tf_op jit(solution)/shard_map/reduce_sum | solution.py:78
  39.4 0.1 div.15
  39.5 1.7 multiply_reduce_fusion.2
  41.2 0.1 rsqrt.12
  41.3 0.0 copy-done.10
  41.3 2.7 add_convert_fusion
  44.1 26.3 %all-gather.3.cloned.1.call-done = bf16[512,2048]{1,0:T(8,128)(2,1)} async-done(((bf16[16,2048]{1,0:T(8,128)(2,1)}), bf16[512,2048]{1,0:T(8,128)(2,1)}) %all-gather.3.cloned.1.call-update) | async-done | bytes 2097168 | tf_op jit(solution)/shard_map/all_gather | solution.py:149
  70.3 0.0 copy-done.13
  70.3 23.4 %multiply_convert_fusion = (bf16[1024,2048]{1,0:T(8,128)(2,1)}, f32[1024,2048]{1,0:T(8,128)}, f32[1024,2048]{1,0:T(8,128)}) fusion(f32[2048]{0:T(1024)S(1)} %copy-done.13, bf16[1024,512]{1,0:T(8,128)(2,1)} %add_convert_fusion, bf16[512,2048]{1,0:T(8,128)(2,1)} %all-gather.3.cloned.1.call-done), kind=kOutput, calls=%fused_computation.52 | convolution fusion | flops 2285895680 | bytes 24125440 | tf_op jit(solution)/shard_map/dot_general | solution.py:83
  93.7 35.0 %all-gather.5.cloned.1.call-done = bf16[2048,512]{1,0:T(8,128)(2,1)} async-done(((bf16[64,512]{1,0:T(8,128)(2,1)}), bf16[2048,512]{1,0:T(8,128)(2,1)}) %all-gather.5.cloned.1.call-update) | async-done | bytes 2097168 | tf_op jit(solution)/shard_map/all_gather | solution.py:150
  128.7 6.9 %fusion.134 = (f32[512]{0:T(512)S(1)}, bf16[1024,512]{1,0:T(8,128)(2,1)}, bf16[1024,512]{1,0:T(8,128)(2,1)S(1)}) fusion(bf16[1,32,32,512]{3,2,1,0:T(8,128)(2,1)} %param.12, f32[512]{0:T(512)S(1)} %copy-done.14, f32[512]{0:T(512)S(1)} %copy-done.9, bf16[1,32,32,512]{3,2,1,0:T(8,128)(2,1)S(1)} %copy-done, bf16[1024,2048]{1,0:T(8,128)(2,1)} %get-tuple-element.87, ...), kind=kOutput, calls=%fused_computation.251 | convolution fusion | flops 2152726016 | bytes 10491904 | tf_op jit(solution)/shard_map/dot_general | solution.py:86
  135.6 0.0 copy-start.2
  135.6 8.0 %fusion.156 = (f32[2048]{0:T(1024)S(1)}, bf16[1024,2048]{1,0:T(8,128)(2,1)S(1)}) fusion(f32[1024,2048]{1,0:T(8,128)S(1)} %copy-done.16, bf16[1024,512]{1,0:T(8,128)(2,1)S(1)} %get-tuple-element.93, bf16[2048,512]{1,0:T(8,128)(2,1)S(1)} %copy-done.12, f32[1024,2048]{1,0:T(8,128)} %get-tuple-element.147, f32[2048]{0:T(1024)S(1)} %copy-done.13), kind=kOutput, calls=%fused_computation.316 | convolution fusion | flops 2181036032 | bytes 24133632 | tf_op jit(solution)/shard_map/dot_general | solution.py:96
  143.7 2.9 multiply_reduce_fusion
  146.5 0.0 copy-start.1
  146.6 6.6 %fusion.129 = (f32[512]{0:T(512)S(1)}, f32[512]{0:T(512)S(1)}, f32[512]{0:T(512)S(1)}, f32[512]{0:T(512)S(1)}, f32[512]{0:T(512)S(1)}, /*index=5*/f32[512]{0:T(5...) fusion(bf16[38,38,512]{2,1,0:T(8,128)(2,1)S(1)} %select_maximum, ...), kind=kLoop, calls=%fused_computation.242 | loop fusion | flops 33545216 | bytes 23123968 | tf_op jit(solution)/shard_map/reduce_sum | solution.py:60
  153.1 0.5 convert_reduce_fusion
  153.6 5.2 fusion.111
  158.8 4.2 fusion.108
  163.4 0.0 copy-start.6
  163.4 0.6 copy-done.6
  164.0 0.0 all-reduce.7.cloned.1.call-update
  164.0 0.0 all-reduce.9.cloned.1.call-start
  164.1 68.0 %all-reduce.7.cloned.1.call-done = f32[7,7,512]{2,1,0:T(8,128)} async-done(((f32[7,7,512]{2,1,0:T(8,128)}), f32[7,7,512]{2,1,0:T(8,128)}) %all-reduce.7.cloned.1.call-update) | async-done | bytes 100368 | tf_op jit(solution)/shard_map/psum | solution.py:178
  232.1 0.0 all-reduce.9.cloned.1.call-update
  232.1 0.3 reduce-scatter.5.cloned.1.call-start
  232.4 6.8 %fusion.157 = f32[2048,512]{1,0:T(8,128)} fusion(bf16[1024,2048]{1,0:T(8,128)(2,1)} %get-tuple-element.87, bf16[1024,512]{1,0:T(8,128)(2,1)} %copy-done.15), kind=kOutput, calls=%fused_computation.317 | convolution fusion | flops 2147483648 | bytes 9437184 | tf_op jit(solution)/shard_map/dot_general | solution.py:93
  239.2 0.0 reduce-scatter.5.cloned.1.call-update
  239.2 0.0 reduce-scatter.3.cloned.1.call-start
  239.3 1.2 copy-done.4
  240.4 6.5 %fusion.136 = f32[512,2048]{1,0:T(8,128)} fusion(bf16[1024,512]{1,0:T(8,128)(2,1)S(1)} %copy-done.4, bf16[1024,2048]{1,0:T(8,128)(2,1)} %copy-done.3), kind=kOutput, calls=%fused_computation.257 | convolution fusion | flops 2147483648 | bytes 9437184 | tf_op jit(solution)/shard_map/dot_general | solution.py:102
  247.0 0.0 reduce-scatter.3.cloned.1.call-update
  247.0 0.1 fusion.151
  247.1 3.4 collective-permute-start.2
  250.5 1.3 collective-permute-start.3
  251.8 0.3 fusion.132
  252.1 37.6 %all-reduce.2 = (f32[512]{0:T(512)S(1)}, f32[512]{0:T(512)S(1)}, f32[512]{0:T(512)S(1)}, f32[2048]{0:T(1024)S(1)}, f32[512]{0:T(512)S(1)}, /*index=5*/f32[512]{0:T(512)S(1)}) all-reduce(f32[512]{0:T(512)S(1)} %get-tuple-element.66, f32[512]{0:T(512)S(1)} %get-tuple-element.11, ...), channel_id=1, replica_groups=mesh['dp'=4,'space'=8] {'space'}, use_global_device_ids=true, to_apply=%region_56.57 | all-reduce | flops 4608 | bytes 36864 | tf_op jit(solution)/shard_map/psum | solution.py:178
  289.7 11.2 %all-reduce.3 = (f32[512]{0:T(512)}, f32[512]{0:T(512)}, f32[512]{0:T(512)}, f32[2048]{0:T(1024)}, f32[512]{0:T(512)}, /*index=5*/f32[512]{0:T(512)}) all-reduce(f32[512]{0:T(512)S(1)} %get-tuple-element.74, f32[512]{0:T(512)S(1)} %get-tuple-element.75, f32[512]{0:T(512)S(1)} %get-tuple-element.76, ...), channel_id=1, replica_groups=mesh['dp'=4,'space'=8] {'dp'}, use_global_device_ids=true, to_apply=%region_57.58 | all-reduce | flops 4608 | bytes 36864 | tf_op jit(solution)/shard_map/psum | solution.py:177
  300.9 0.0 collective-permute-done.2
  300.9 0.0 collective-permute-done.3
  300.9 0.8 select_maximum_fusion
  301.7 17.8 %fusion.149 = bf16[1,32,32,512]{3,2,1,0:T(8,128)(2,1)} fusion(bf16[38,38,512]{2,1,0:T(8,128)(2,1)S(1)} %select_maximum_fusion, f32[512]{0:T(512)S(1)} %bitcast.311, f32[512]{0:T(512)S(1)} %bitcast.313, f32[512]{0:T(512)S(1)} %bitcast.219, f32[512]{0:T(512)S(1)} %bitcast.221, f32[512]{0:T(512)S(1)} %bitcast.223, f32[512]{0:T(512)S(1)} %bitcast.225, ...), kind=kLoop, calls=%fused_computation.299 | loop fusion | flops 87556096 | bytes 47482880 | tf_op jit(solution)/shard_map/broadcast_in_dim | solution.py:198
  319.5 93.1 %reduce-scatter.5.cloned.1.call-done = f32[64,512]{1,0:T(8,128)} async-done(((f32[2048,512]{1,0:T(8,128)}), f32[64,512]{1,0:T(8,128)}) %reduce-scatter.5.cloned.1.call-update) | async-done | bytes 131088 | tf_op jit(solution)/shard_map/reduce_scatter | solution.py:194
  412.5 143.8 %reduce-scatter.3.cloned.1.call-done = f32[16,2048]{1,0:T(8,128)} async-done(((f32[512,2048]{1,0:T(8,128)}), f32[16,2048]{1,0:T(8,128)}) %reduce-scatter.3.cloned.1.call-update) | async-done | bytes 131088 | tf_op jit(solution)/shard_map/reduce_scatter | solution.py:193
  556.3 1.6 copy.30
  (40 shorter events, 0.3 us)
Async XLA Ops:
  7.2 15.7 %copy-start = (bf16[1,32,32,512]{3,2,1,0:T(8,128)(2,1)S(1)}, bf16[1,32,32,512]{3,2,1,0:T(8,128)(2,1)}, u32[]{:S(2)}) copy-start(bf16[1,32,32,512]{3,2,1,0:T(8,128)(2,1)} %param.11) | copy-start | bytes 3145732
  7.2 15.7 %copy-start.8 = (f32[512]{0:T(512)S(1)}, f32[512]{0:T(512)}, u32[]{:S(2)}) copy-start(f32[512]{0:T(512)} %param.14) | copy-start | bytes 6148
  7.2 63.1 %all-gather.3.cloned.1.call-start = ((), (), s32[]{:S(2)}) async-start(), calls=%async_computation.2 | async-start | bytes 2162688 | tf_op jit(solution)/shard_map/all_gather | solution.py:149
  7.9 120.8 %all-gather.5.cloned.1.call-start = ((), (), s32[]{:S(2)}) async-start(), calls=%async_computation.3 | async-start | bytes 2162688 | tf_op jit(solution)/shard_map/all_gather | solution.py:150
  9.1 9.5 %collective-permute-start = (bf16[32,3,512]{2,1,0:T(4,128)(2,1)S(1)}, bf16[32,3,512]{2,1,0:T(4,128)(2,1)S(1)}, u32[]{:S(2)}, u32[]{:S(2)}) collective-permute-start(bf16[32,3,512]{2,1,0:T(4,128)(2,1)S(1)} %get-tuple-element.96), channel_id=1, source_target_pairs={{0,1},{1,2},{2,3},{3,4},{4,5},{5,6},{6,7},{8,9},{9,10},{10,11},{11... | collective-permute-start | bytes 294920 | tf_op jit(solution)/shard_map/ppermute | solution.py:17
  14.0 6.9 %collective-permute-start.1 = (bf16[32,3,512]{2,1,0:T(4,128)(2,1)S(1)}, bf16[32,3,512]{2,1,0:T(4,128)(2,1)S(1)}, u32[]{:S(2)}, u32[]{:S(2)}) collective-permute-start(bf16[32,3,512]{2,1,0:T(4,128)(2,1)S(1)} %get-tuple-element.97), channel_id=1, source_target_pairs={{1,0},{2,1},{3,2},{4,3},{5,4},{6,5},{7,6},{9,8},{10,9},{11,10},{12... | collective-permute-start | bytes 294920 | tf_op jit(solution)/shard_map/ppermute | solution.py:18
  15.3 216.7 %all-reduce.7.cloned.1.call-start = ((), (), s32[]{:S(2)}) async-start(), calls=%async_computation.4 | async-start | bytes 229376 | tf_op jit(solution)/shard_map/psum | solution.py:178
  22.9 18.4 %copy-start.7 = (f32[512]{0:T(512)S(1)}, f32[512]{0:T(512)}, u32[]{:S(2)}) copy-start(f32[512]{0:T(512)} %param.15) | copy-start | bytes 6148
  22.9 18.4 %copy-start.10 = (f32[512]{0:T(512)S(1)}, f32[512]{0:T(512)}, u32[]{:S(2)}) copy-start(f32[512]{0:T(512)} %param.16) | copy-start | bytes 6148
  39.4 30.9 %copy-start.13 = (f32[2048]{0:T(1024)S(1)}, f32[2048]{0:T(1024)}, u32[]{:S(2)}) copy-start(f32[2048]{0:T(1024)} %param.18) | copy-start | bytes 24580
  44.1 84.7 %copy-start.9 = (f32[512]{0:T(512)S(1)}, f32[512]{0:T(512)}, u32[]{:S(2)}) copy-start(f32[512]{0:T(512)} %param.21) | copy-start | bytes 6148
  44.1 84.7 %copy-start.14 = (f32[512]{0:T(512)S(1)}, f32[512]{0:T(512)}, u32[]{:S(2)}) copy-start(f32[512]{0:T(512)} %param.20) | copy-start | bytes 6148
  128.7 6.9 %copy-start.12 = (bf16[2048,512]{1,0:T(8,128)(2,1)S(1)}, bf16[2048,512]{1,0:T(8,128)(2,1)}, u32[]{:S(2)}) copy-start(bf16[2048,512]{1,0:T(8,128)(2,1)} %all-gather.5.cloned.1.call-done) | copy-start | bytes 6291460
  128.7 6.9 %copy-start.16 = (f32[1024,2048]{1,0:T(8,128)S(1)}, f32[1024,2048]{1,0:T(8,128)}, u32[]{:S(2)}) copy-start(f32[1024,2048]{1,0:T(8,128)} %get-tuple-element.88) | copy-start | bytes 25165828
  135.6 8.0 %copy-start.15 = (bf16[1024,512]{1,0:T(8,128)(2,1)}, bf16[1024,512]{1,0:T(8,128)(2,1)S(1)}, u32[]{:S(2)}) copy-start(bf16[1024,512]{1,0:T(8,128)(2,1)S(1)} %get-tuple-element.93) | copy-start | bytes 3145732
  135.6 8.0 %copy-start.2 = (bf16[32,32,512]{2,1,0:T(8,128)(2,1)S(1)}, bf16[32,32,512]{2,1,0:T(8,128)(2,1)}, u32[]{:S(2)}) copy-start(bf16[32,32,512]{2,1,0:T(8,128)(2,1)} %get-tuple-element.90) | copy-start | bytes 3145732
  135.6 8.0 %copy-start.11 = (bf16[512,2048]{1,0:T(8,128)(2,1)S(1)}, bf16[512,2048]{1,0:T(8,128)(2,1)}, u32[]{:S(2)}) copy-start(bf16[512,2048]{1,0:T(8,128)(2,1)} %all-gather.3.cloned.1.call-done) | copy-start | bytes 6291460
  143.6 2.9 copy-start.3
  146.5 6.6 %copy-start.1 = (bf16[1,32,32,512]{3,2,1,0:T(8,128)(2,1)S(1)}, bf16[1,32,32,512]{3,2,1,0:T(8,128)(2,1)}, u32[]{:S(2)}) copy-start(bf16[1,32,32,512]{3,2,1,0:T(8,128)(2,1)} %param.11) | copy-start | bytes 3145732
  163.4 0.6 copy-start.6
  164.0 155.4 %all-reduce.9.cloned.1.call-start = ((), (), s32[]{:S(2)}) async-start(), calls=%async_computation.5 | async-start | bytes 229376 | tf_op jit(solution)/shard_map/psum | solution.py:177
  232.1 180.4 %reduce-scatter.5.cloned.1.call-start = ((), (), s32[]{:S(2)}) async-start(), calls=%async_computation.7 | async-start | bytes 4325376 | tf_op jit(solution)/shard_map/reduce_scatter | solution.py:194
  239.2 1.2 copy-start.4
  239.2 317.1 %reduce-scatter.3.cloned.1.call-start = ((), (), s32[]{:S(2)}) async-start(), calls=%async_computation.6 | async-start | bytes 4325376 | tf_op jit(solution)/shard_map/reduce_scatter | solution.py:193
  247.0 4.8 copy-start.5
  247.1 53.8 %collective-permute-start.2 = (bf16[32,3,512]{2,1,0:T(4,128)(2,1)S(1)}, bf16[32,3,512]{2,1,0:T(4,128)(2,1)S(1)}, u32[]{:S(2)}, u32[]{:S(2)}) collective-permute-start(bf16[32,3,512]{2,1,0:T(4,128)(2,1)S(1)} %get-tuple-element.94), channel_id=1, source_target_pairs={{0,1},{1,2},{2,3},{3,4},{4,5},{5,6},{6,7},{8,9},{9,10},{10,11},{11... | collective-permute-start | bytes 294920 | tf_op jit(solution)/shard_map/ppermute | solution.py:17
  250.5 50.4 %collective-permute-start.3 = (bf16[32,3,512]{2,1,0:T(4,128)(2,1)S(1)}, bf16[32,3,512]{2,1,0:T(4,128)(2,1)S(1)}, u32[]{:S(2)}, u32[]{:S(2)}) collective-permute-start(bf16[32,3,512]{2,1,0:T(4,128)(2,1)S(1)} %get-tuple-element.95), channel_id=1, source_target_pairs={{1,0},{2,1},{3,2},{4,3},{5,4},{6,5},{7,6},{9,8},{10,9},{11,10},{12... | collective-permute-start | bytes 294920 | tf_op jit(solution)/shard_map/ppermute | solution.py:18
Sparse Core Ops, SparseCore 0:
  11.0 59.2 all-gather.2
  73.3 55.3 all-gather.4
  164.2 67.8 all-reduce.6
  234.4 29.7 all-reduce.8
  266.9 145.5 reduce-scatter.4
  415.2 141.0 reduce-scatter.2
